TPU v7x, 512 devices: a whole 4x8x8 slice. The times are simulated.
512 devices in a mesh: dp: 16 (over y, core), mp: 32 (over x, z).
Axes of the slice: x: 4, y: 8, z: 8, core: 2. Of those that a mesh axis runs over, the one named last changes fastest.
Arguments:
- packed_rows: bfloat16 [16384, 6144], P(('dp', 'mp')), may hold values from -6 to 6
- dest_group: int32 [16384], P(('dp', 'mp')), may hold values from 0 to 15, as said below
- dest_slot: int32 [16384], P(('dp', 'mp')), may hold values from 0 to 31, as said below
- image_ids: int32 [16, 1024], P('dp', 'mp'), may hold values from 0 to 15, never falling along the last dimension, each value on 1 to 512 neighbouring positions
- ln_gain: float32 [6144], replicated, may hold values from 0.1 to 1.9
- qkv_weight: bfloat16 [3, 6144, 4096], P(None, None, 'mp'), may hold values from -0.078125 to 0.078125
- qk_gain: float32 [2, 4096], P(None, 'mp'), may hold values from 0.6 to 8
Outputs:
- attended: bfloat16 [16384, 4096], P(('dp', 'mp'))
Inputs may be any that keep to these rules, and one draw needn't show every extreme that they name: `dest_group`: rows of the loader at mp index m go to tokens m * 32 to (m + 1) * 32 - 1 of their group. Each loader device sends at most 4 rows to one group, and in every draw some loader device sends exactly 4 rows to one group. `dest_slot`: together with dest_group, every slot of every receiving device gets exactly one row.
All inputs are finite; a program needn't handle non-finite values.
Results may differ from a plain program's by a relative error of at most 0.022.
The roundings to bfloat16 on the way count: a program that leaves them out, or rounds other values in their place, can miss the bound.
Values may be sent and summed in bfloat16 or wider, within the bound.
No kernel may reach another device: no remote copies, remote signals or barrier semaphores. Data moves between devices by JAX's collectives and lax.ppermute only.
A program may use at most 64 MiB of HBM per device.

v0:
```python
import jax
import jax.numpy as jnp
from jax import lax
from jax.sharding import PartitionSpec as P

HD = 128


def norm_rows(rows, gain):
    values = rows.astype(jnp.float32)
    mean = jnp.mean(values, axis=-1, keepdims=True)
    centered = values - mean
    spread = jnp.mean(centered * centered, axis=-1, keepdims=True)
    return (centered * lax.rsqrt(spread + 1e-06) * gain).astype(jnp.bfloat16)


def local(packed_rows, dest_group, dest_slot, image_ids, ln_gain, qkv_weight, qk_gain):
    normed = norm_rows(packed_rows, ln_gain)
    tok_rows = packed_rows.shape[0]
    width = packed_rows.shape[1]
    n_groups = lax.axis_size("dp")
    capacity = max(2, 2 * tok_rows // n_groups)
    positions = jnp.arange(tok_rows, dtype=jnp.int32)
    earlier = (dest_group[:, None] == dest_group[None, :]) & (
        positions[None, :] < positions[:, None]
    )
    rank = jnp.sum(earlier.astype(jnp.int32), axis=1)
    send_rows = (
        jnp.zeros((n_groups, capacity, width), jnp.bfloat16).at[dest_group, rank].set(normed)
    )
    send_slots = (
        jnp.full((n_groups, capacity), -1.0, jnp.bfloat16)
        .at[dest_group, rank]
        .set(dest_slot.astype(jnp.bfloat16))
    )
    got_rows, got_slots = (
        lax.all_to_all(send_rows, "dp", split_axis=0, concat_axis=0, tiled=True),
        lax.all_to_all(send_slots, "dp", split_axis=0, concat_axis=0, tiled=True),
    )
    flat_rows = got_rows.reshape(n_groups * capacity, width)
    flat_slots = got_slots.reshape(n_groups * capacity).astype(jnp.float32)
    placing = (flat_slots[None, :] == positions[:, None].astype(jnp.float32)).astype(jnp.bfloat16)
    tokens = jnp.dot(placing, flat_rows, preferred_element_type=jnp.float32).astype(jnp.bfloat16)
    group_rows, group_ids = (
        lax.all_gather(tokens, "mp", axis=0, tiled=True),
        lax.all_gather(image_ids[0].astype(jnp.bfloat16), "mp", axis=0, tiled=True),
    )
    count = group_rows.shape[0]
    heads = qkv_weight.shape[2] // HD
    projected = jnp.einsum(
        "td,kdc->ktc", group_rows, qkv_weight, preferred_element_type=jnp.float32
    )
    query_n = norm_rows(projected[0].reshape(count, heads, HD), qk_gain[0].reshape(heads, HD))
    key_n = norm_rows(projected[1].reshape(count, heads, HD), qk_gain[1].reshape(heads, HD))
    value = projected[2].astype(jnp.bfloat16).reshape(count, heads, HD)
    scores = jnp.einsum(
        "qhc,khc->hqk", query_n, key_n, preferred_element_type=jnp.float32
    ) * HD ** (-0.5)
    image_f = group_ids.astype(jnp.float32)
    same = image_f[:, None] == image_f[None, :]
    masked = jnp.where(same[None], scores, -1e30)
    top = jnp.max(masked, axis=-1, keepdims=True)
    weights = jnp.exp(masked - top)
    probs = (weights / jnp.sum(weights, axis=-1, keepdims=True)).astype(jnp.bfloat16)
    result = jnp.einsum("hqk,khc->qhc", probs, value, preferred_element_type=jnp.float32)
    result = result.astype(jnp.bfloat16).reshape(count, heads * HD)
    return lax.all_to_all(result, "mp", split_axis=0, concat_axis=1, tiled=True)


def solution(mesh):
    return jax.shard_map(
        local,
        mesh=mesh,
        in_specs=(
            P(("dp", "mp"), None),
            P(("dp", "mp")),
            P(("dp", "mp")),
            P("dp", "mp"),
            P(),
            P(None, None, "mp"),
            P(None, "mp"),
        ),
        out_specs=P(("dp", "mp"), None),
        check_vma=False,
    )
```

profile of v0, /device:TPU:8, one launch (start us, length us, event | category | flops | bytes accessed | tf_op | source)
XLA Modules:
  0.0 229.7 jit_solution(2317695493599553311)
XLA Ops:
  6.5 0.9 convert_reduce_fusion.1
  7.4 0.7 fusion.39
  8.1 0.7 convert_element_type.105
  8.8 2.1 scatter_fusion
  10.8 0.7 copy.22
  11.5 9.1 %all-to-all-start = ((bf16[16,1,4]{2,1,0:T(2,128)(2,1)}), bf16[16,1,4]{2,1,0:T(2,128)(2,1)S(1)}, u32[]{:S(2)}, u32[]{:S(2)}) async-start(bf16[16,1,4]{2,1,0:T(2,128)(2,1)} %copy.22), calls=%async_computation | async-start | bytes 16384 | tf_op jit(solution)/shard_map/all_to_all | solution.py:38
  20.6 1.2 convert_reduce_fusion
  21.8 1.3 fusion.7
  23.1 1.2 fusion.9
  24.3 1.2 broadcast_in_dim.11
  25.5 10.3 %scatter_fusion.1 = bf16[16,4,6144]{2,1,0:T(4,128)(2,1)} fusion(bf16[16,4,6144]{2,1,0:T(4,128)(2,1)} %broadcast_in_dim.11, s32[32]{0:T(128)S(1)} %fusion.39, bf16[32,6144]{1,0:T(8,128)(2,1)S(1)} %fusion.9), kind=kCustom, calls=%fused_computation.1 | custom fusion | bytes 1179904 | tf_op jit(solution)/shard_map/scatter | solution.py:29
  35.7 7.2 %all-to-all-start.1 = ((bf16[16,4,6144]{2,1,0:T(4,128)(2,1)}), bf16[16,4,6144]{2,1,0:T(4,128)(2,1)S(1)}, u32[]{:S(2)}, u32[]{:S(2)}) async-start(bf16[16,4,6144]{2,1,0:T(4,128)(2,1)} %scatter_fusion.1), calls=%async_computation.1 | async-start | bytes 1572864 | tf_op jit(solution)/shard_map/all_to_all | solution.py:37
  43.1 18.9 %all-to-all-done.1 = bf16[16,4,6144]{2,1,0:T(4,128)(2,1)S(1)} async-done(((bf16[16,4,6144]{2,1,0:T(4,128)(2,1)}), bf16[16,4,6144]{2,1,0:T(4,128)(2,1)S(1)}, u32[]{:S(2)}, u32[]{:S(2)}) %all-to-all-start.1) | async-done | bytes 786464 | tf_op jit(solution)/shard_map/all_to_all | solution.py:37
  62.2 1.1 convolution_convert_fusion
  63.4 6.6 %copy.23 = bf16[3,6144,128]{1,2,0:T(8,128)(2,1)} copy(bf16[3,6144,128]{2,1,0:T(8,128)(2,1)} %param.12) | data formatting | bytes 9437184 | tf_op args[5]
  70.0 1.3 dynamic-slice
  72.2 80.0 %all-reduce = bf16[1024]{0:T(1024)(128)(2,1)S(1)} all-reduce(bf16[1024]{0:T(1024)(128)(2,1)S(1)} %dynamic-update-slice), channel_id=2, replica_groups=mesh['dp'=16,'mp'=32] {'mp'}, use_global_device_ids=true, to_apply=%add | all-reduce | flops 1024 | bytes 4096
  152.3 39.4 %all-gather.3.cloned.1.call-done = bf16[1024,6144]{1,0:T(8,128)(2,1)} async-done(((bf16[32,6144]{1,0:T(8,128)(2,1)}), bf16[1024,6144]{1,0:T(8,128)(2,1)}) %all-gather.3.cloned.1.call-update) | async-done | bytes 12582928 | tf_op jit(solution)/shard_map/all_gather | solution.py:45
  191.7 9.4 %fusion.42 = f32[1024,384]{0,1:S(1)} fusion(bf16[1024,6144]{1,0:T(8,128)(2,1)} %all-gather.3.cloned.1.call-done, bf16[6144,384]{0,1:T(8,128)(2,1)} %bitcast.92), kind=kOutput, calls=%fused_computation.73 | convolution fusion | flops 4831838208 | bytes 18874368
  201.4 1.0 fusion.1
  202.3 1.0 fusion
  203.4 1.4 fusion.4
  204.9 17.2 %all_to_all.33 = bf16[32,32,128]{2,1,0:T(8,128)(2,1)S(1)} all-to-all(bf16[32,32,128]{2,1,0:T(8,128)(2,1)S(1)} %bitcast.97), channel_id=1, replica_groups=mesh['dp'=16,'mp'=32] {'mp'}, dimensions={0} | all-to-all | bytes 524288 | tf_op jit(solution)/shard_map/all_to_all | solution.py:67
  222.1 0.7 copy_bitcast_fusion
  (25 shorter events, 1.0 us)
Async XLA Ops:
  11.5 24.2 %all-to-all-start = ((bf16[16,1,4]{2,1,0:T(2,128)(2,1)}), bf16[16,1,4]{2,1,0:T(2,128)(2,1)S(1)}, u32[]{:S(2)}, u32[]{:S(2)}) async-start(bf16[16,1,4]{2,1,0:T(2,128)(2,1)} %copy.22), calls=%async_computation | async-start | bytes 16384 | tf_op jit(solution)/shard_map/all_to_all | solution.py:38
  35.7 26.3 %all-to-all-start.1 = ((bf16[16,4,6144]{2,1,0:T(4,128)(2,1)}), bf16[16,4,6144]{2,1,0:T(4,128)(2,1)S(1)}, u32[]{:S(2)}, u32[]{:S(2)}) async-start(bf16[16,4,6144]{2,1,0:T(4,128)(2,1)} %scatter_fusion.1), calls=%async_computation.1 | async-start | bytes 1572864 | tf_op jit(solution)/shard_map/all_to_all | solution.py:37
  43.0 148.7 %all-gather.3.cloned.1.call-start = ((), (), s32[]{:S(2)}) async-start(), calls=%async_computation.3 | async-start | bytes 12976128 | tf_op jit(solution)/shard_map/all_gather | solution.py:45
  63.4 8.6 %copy-start.1 = (s32[1,32]{1,0:T(1,128)S(1)}, s32[1,32]{1,0:T(1,128)}, u32[]{:S(2)}) copy-start(s32[1,32]{1,0:T(1,128)} %param.10) | copy-start | bytes 388
  63.4 88.9 %copy-start = (f32[2,128]{1,0:T(2,128)S(1)}, f32[2,128]{1,0:T(2,128)}, u32[]{:S(2)}) copy-start(f32[2,128]{1,0:T(2,128)} %param.13) | copy-start | bytes 3076
Sparse Core Ops, SparseCore 0:
  63.5 128.1 all-gather.2
where the time goes:
time: 230 us
  blocking collectives  97.2 us (42%)
  waiting for transfers between devices  58.3 us (25%)
  local copies, waits for them, and re-layouts  23.5 us (10%)
  starting transfers between devices  16.4 us (7%)
  between operations  14.2 us (6%)
  matrix products  12.9 us (6%)
  other arithmetic  7.15 us (3%)
    unnamed x1, blocking collectives  80 us
    all_gather x1, waiting for transfers between devices, local(): lax.all_gather(tokens, 'mp', axis=0, tiled=True)  39.4 us
    all_to_all x1, waiting for transfers between devices, local(): lax.all_to_all(send_rows, 'dp', split_axis=0, concat_axis=0, tiled=True)  18.9 us
    all_to_all x1, blocking collectives, local(): return lax.all_to_all(result, 'mp', split_axis=0, concat_axis=1, tiled=True)  17.2 us
    scatter x1, local copies, waits for them, and re-layouts, local(): jnp.zeros((n_groups, capacity, width), jnp.bfloat16).at[dest_group, rank]  10.3 us
    unnamed x1, matrix products  9.44 us
    all_to_all x1, starting transfers between devices, local(): lax.all_to_all(send_slots, 'dp', split_axis=0, concat_axis=0, tiled=True)  9.09 us
    unnamed x8, local copies, waits for them, and re-layouts  8.16 us
  transfers between devices with their start and end apart: 3, of which 2 were waited for; matrix products, arithmetic and copies ran while one was open for 10% of the time, Pallas kernels for 0%

commit v1 on v0

--- a/solution.py
+++ b/solution.py
@@ -42,7 +42,9 @@
     placing = (flat_slots[None, :] == positions[:, None].astype(jnp.float32)).astype(jnp.bfloat16)
     tokens = jnp.dot(placing, flat_rows, preferred_element_type=jnp.float32).astype(jnp.bfloat16)
     group_rows, group_ids = (
-        lax.all_gather(tokens, "mp", axis=0, tiled=True),
+        jnp.concatenate(
+            lax.all_to_all(jnp.stack([tokens] * lax.axis_size("mp")), "mp", 0, 0), axis=0
+        ),
         lax.all_gather(image_ids[0].astype(jnp.bfloat16), "mp", axis=0, tiled=True),
     )
     count = group_rows.shape[0]

time: 230 us -> 472 us (2.05)
  the two profiles are of different devices: /device:TPU:8 before, /device:TPU:24 now
where the time goes in v1:
time: 472 us; the launch traced here: 471 us
  blocking collectives  373 us (79%)
  local copies, waits for them, and re-layouts  29.7 us (6%)
  starting transfers between devices  27.8 us (6%)
  waiting for transfers between devices  20.5 us (4%)
  matrix products  12.1 us (3%)
  other arithmetic  7.15 us (2%)
    unnamed x1, blocking collectives  360 us
    all_to_all x1, waiting for transfers between devices, local(): lax.all_to_all(send_rows, 'dp', split_axis=0, concat_axis=0, tiled=True)  20.5 us
    all_to_all x1, blocking collectives, local(): return lax.all_to_all(result, 'mp', split_axis=0, concat_axis=1, tiled=True)  13.8 us
    all_to_all x1, starting transfers between devices, local(): lax.all_to_all(jnp.stack([tokens] * lax.axis_size('mp')), 'mp', 0, 0)  11.7 us
    scatter x1, local copies, waits for them, and re-layouts, local(): jnp.zeros((n_groups, capacity, width), jnp.bfloat16).at[dest_group, rank]  10.3 us
    unnamed x1, matrix products  9.45 us
  transfers between devices with their start and end apart: 3, of which 1 were waited for; matrix products, arithmetic and copies ran while one was open for 5% of the time, Pallas kernels for 0%

profile of v1, /device:TPU:24, one launch (start us, length us, event | category | flops | bytes accessed | tf_op | source)
XLA Modules:
  0.0 471.4 jit_solution(10508030553364314464)
XLA Ops:
  0.0 0.9 convert_reduce_fusion.1
  0.9 0.7 fusion.39
  1.6 0.7 convert_element_type.105
  2.2 2.1 scatter_fusion
  4.3 0.7 copy.22
  5.0 8.9 %all-to-all-start = ((bf16[16,1,4]{2,1,0:T(2,128)(2,1)}), bf16[16,1,4]{2,1,0:T(2,128)(2,1)S(1)}, u32[]{:S(2)}, u32[]{:S(2)}) async-start(bf16[16,1,4]{2,1,0:T(2,128)(2,1)} %copy.22), calls=%async_computation | async-start | bytes 16384 | tf_op jit(solution)/shard_map/all_to_all | solution.py:38
  13.9 1.2 convert_reduce_fusion
  15.1 1.3 fusion.7
  16.3 1.2 fusion.9
  17.5 1.2 broadcast_in_dim.11
  18.7 10.3 %scatter_fusion.1 = bf16[16,4,6144]{2,1,0:T(4,128)(2,1)} fusion(bf16[16,4,6144]{2,1,0:T(4,128)(2,1)} %broadcast_in_dim.11, s32[32]{0:T(128)S(1)} %fusion.39, bf16[32,6144]{1,0:T(8,128)(2,1)S(1)} %fusion.9), kind=kCustom, calls=%fused_computation.1 | custom fusion | bytes 1179904 | tf_op jit(solution)/shard_map/scatter | solution.py:29
  29.1 7.1 %all-to-all-start.1 = ((bf16[16,4,6144]{2,1,0:T(4,128)(2,1)}), bf16[16,4,6144]{2,1,0:T(4,128)(2,1)S(1)}, u32[]{:S(2)}, u32[]{:S(2)}) async-start(bf16[16,4,6144]{2,1,0:T(4,128)(2,1)} %scatter_fusion.1), calls=%async_computation.1 | async-start | bytes 1572864 | tf_op jit(solution)/shard_map/all_to_all | solution.py:37
  36.3 20.5 %all-to-all-done.1 = bf16[16,4,6144]{2,1,0:T(4,128)(2,1)S(1)} async-done(((bf16[16,4,6144]{2,1,0:T(4,128)(2,1)}), bf16[16,4,6144]{2,1,0:T(4,128)(2,1)S(1)}, u32[]{:S(2)}, u32[]{:S(2)}) %all-to-all-start.1) | async-done | bytes 786464 | tf_op jit(solution)/shard_map/all_to_all | solution.py:37
  57.3 6.0 %stack.2 = bf16[32,32,6144]{2,1,0:T(8,128)(2,1)} broadcast(bf16[32,6144]{1,0:T(8,128)(2,1)S(1)} %convolution_convert_fusion), dimensions={1,2} | broadcast | bytes 12976128 | tf_op jit(solution)/shard_map/stack | solution.py:46
  63.4 11.7 %all-to-all-start.2 = ((bf16[32,32,6144]{2,1,0:T(8,128)(2,1)}), bf16[32,32,6144]{2,1,0:T(8,128)(2,1)}, u32[]{:S(2)}, u32[]{:S(2)}) async-start(bf16[32,32,6144]{2,1,0:T(8,128)(2,1)} %stack.2), calls=%async_computation.2 | async-start | bytes 25165824 | tf_op jit(solution)/shard_map/all_to_all | solution.py:46
  75.2 6.7 %copy.23 = bf16[3,6144,128]{1,2,0:T(8,128)(2,1)} copy(bf16[3,6144,128]{2,1,0:T(8,128)(2,1)} %param.12) | data formatting | bytes 9437184 | tf_op args[5]
  81.8 1.3 dynamic-slice
  84.0 359.6 %all-reduce = bf16[1024]{0:T(1024)(128)(2,1)S(1)} all-reduce(bf16[1024]{0:T(1024)(128)(2,1)S(1)} %dynamic-update-slice), channel_id=2, replica_groups=mesh['dp'=16,'mp'=32] {'mp'}, use_global_device_ids=true, to_apply=%add | all-reduce | flops 1024 | bytes 4096
  443.6 9.5 %fusion.42 = f32[1024,384]{0,1:S(1)} fusion(bf16[1024,6144]{1,0:T(8,128)(2,1)} %bitcast.4, bf16[6144,384]{0,1:T(8,128)(2,1)} %bitcast.93), kind=kOutput, calls=%fused_computation.73 | convolution fusion | flops 4831838208 | bytes 18874368
  453.3 1.0 fusion.1
  454.3 1.0 fusion
  455.3 1.4 fusion.4
  456.9 13.8 %all_to_all.38 = bf16[32,32,128]{2,1,0:T(8,128)(2,1)S(1)} all-to-all(bf16[32,32,128]{2,1,0:T(8,128)(2,1)S(1)} %bitcast.98), channel_id=1, replica_groups=mesh['dp'=16,'mp'=32] {'mp'}, dimensions={0} | all-to-all | bytes 524288 | tf_op jit(solution)/shard_map/all_to_all | solution.py:69
  470.7 0.7 copy_bitcast_fusion
  (25 shorter events, 1.3 us)
Async XLA Ops:
  5.0 24.1 %all-to-all-start = ((bf16[16,1,4]{2,1,0:T(2,128)(2,1)}), bf16[16,1,4]{2,1,0:T(2,128)(2,1)S(1)}, u32[]{:S(2)}, u32[]{:S(2)}) async-start(bf16[16,1,4]{2,1,0:T(2,128)(2,1)} %copy.22), calls=%async_computation | async-start | bytes 16384 | tf_op jit(solution)/shard_map/all_to_all | solution.py:38
  29.1 27.8 %all-to-all-start.1 = ((bf16[16,4,6144]{2,1,0:T(4,128)(2,1)}), bf16[16,4,6144]{2,1,0:T(4,128)(2,1)S(1)}, u32[]{:S(2)}, u32[]{:S(2)}) async-start(bf16[16,4,6144]{2,1,0:T(4,128)(2,1)} %scatter_fusion.1), calls=%async_computation.1 | async-start | bytes 1572864 | tf_op jit(solution)/shard_map/all_to_all | solution.py:37
  63.4 380.2 %all-to-all-start.2 = ((bf16[32,32,6144]{2,1,0:T(8,128)(2,1)}), bf16[32,32,6144]{2,1,0:T(8,128)(2,1)}, u32[]{:S(2)}, u32[]{:S(2)}) async-start(bf16[32,32,6144]{2,1,0:T(8,128)(2,1)} %stack.2), calls=%async_computation.2 | async-start | bytes 25165824 | tf_op jit(solution)/shard_map/all_to_all | solution.py:46
  75.1 8.6 %copy-start.1 = (s32[1,32]{1,0:T(1,128)S(1)}, s32[1,32]{1,0:T(1,128)}, u32[]{:S(2)}) copy-start(s32[1,32]{1,0:T(1,128)} %param.10) | copy-start | bytes 388
  75.1 368.5 %copy-start = (f32[2,128]{1,0:T(2,128)S(1)}, f32[2,128]{1,0:T(2,128)}, u32[]{:S(2)}) copy-start(f32[2,128]{1,0:T(2,128)} %param.13) | copy-start | bytes 3076
